TPU v7x, 256 devices: a whole 4x4x8 slice. The times are simulated.
256 devices in a mesh: section: 16 (over z_lo, x), sp: 16 (over y, z_hi, core).
Axes of the slice: x: 4, y: 4, z: 8 (z_hi: 2, z_lo: 4; z = z_hi * 4 + z_lo), core: 2. Of those that a mesh axis runs over, the one named last changes fastest.
Arguments:
- latents: bfloat16 [4, 256, 3072], P(None, 'sp'), may hold values from -6 to 6
- in_flight: bfloat16 [16, 256, 3072], P('section', 'sp'), may hold values from -6 to 6
- modulation: float32 [16, 3, 3072], P('section'), may hold values from -3 to 3
- w_qkv: bfloat16 [16, 3072, 3, 2048], P('section', None, None, 'sp'), may hold values from -0.109375 to 0.109375
- w_expand: bfloat16 [16, 3072, 10240], P('section', None, 'sp'), may hold values from -0.109375 to 0.109375
- qk_gain: float32 [16, 2, 128], P('section'), may hold values from 0.3 to 3
- w_out: bfloat16 [16, 2048, 3072], P('section', 'sp'), may hold values from -0.0546875 to 0.0546875
- w_contract: bfloat16 [16, 10240, 3072], P('section', 'sp'), may hold values from -0.0546875 to 0.0546875
- stale_kv: bfloat16 [16, 2, 1024, 2048], P('section', None, None, 'sp'), may hold values from -400 to 400, as said below
Outputs:
- section_out: bfloat16 [16, 4, 256, 3072], P('section', None, 'sp')
- fresh_kv: bfloat16 [16, 4, 2, 256, 2048], P('section', None, None, None, 'sp')
Inputs may be any that keep to these rules, and one draw needn't show every extreme that they name: `stale_kv`: entry 0 holds keys and entry 1 values; patch m occupies rows m * 256 to (m + 1) * 256 - 1.
All inputs are finite; a program needn't handle non-finite values.
Results may differ from a plain program's by a relative error of at most 0.03.
Values may be sent and summed in bfloat16 or wider, within the bound.
A program may use at most 128 MiB of HBM per device.

v0:
```python
import jax
import jax.numpy as jnp
from jax import lax
from jax.sharding import PartitionSpec as P


def from_behind(block, axis, distance):
    devices = range(lax.axis_size(axis))
    route = [(i - distance, i) for i in devices if i - distance in devices]
    return lax.ppermute(block, axis, route)


def modulate(inputs, shift_row, scale_row):
    values = inputs.astype(jnp.float32)
    average = jnp.mean(values, axis=-1, keepdims=True)
    centred = values - average
    variance = jnp.mean(centred * centred, axis=-1, keepdims=True)
    normed = centred * lax.rsqrt(variance + 1e-06)
    return (normed * (1.0 + scale_row) + shift_row).astype(jnp.bfloat16)


def head_norm(values, gain_row):
    mean_square = jnp.mean(values * values, axis=-1, keepdims=True)
    return (values * lax.rsqrt(mean_square + 1e-06) * gain_row).astype(jnp.bfloat16)


def attend(queries, all_keys, all_values, head_dim):
    scores = jnp.einsum(
        "qhd,khd->hqk", queries, all_keys, preferred_element_type=jnp.float32
    ) * head_dim ** (-0.5)
    highest = jnp.max(scores, axis=-1, keepdims=True)
    weights = jnp.exp(scores - highest)
    totals = jnp.sum(weights, axis=-1, keepdims=True)
    shares = (weights / totals).astype(jnp.bfloat16)
    return jnp.einsum(
        "hqk,khd->qhd", shares, all_values, preferred_element_type=jnp.float32
    ).astype(jnp.bfloat16)


def local(latents, in_flight, modulation, w_qkv, w_expand, qk_gain, w_out, w_contract, stale_kv):
    section_index = lax.axis_index("section")
    micro_count = latents.shape[0]
    width = latents.shape[2]
    head_dim = qk_gain.shape[2]
    local_cols = w_qkv.shape[3]
    local_heads = local_cols // head_dim
    shift_row = modulation[0, 0]
    scale_row = modulation[0, 1]
    gate_row = modulation[0, 2]
    proj_weight = w_qkv[0].reshape(width, 3 * local_cols)
    expand_weight = w_expand[0]
    out_weight = w_out[0]
    contract_weight = w_contract[0]
    stale_local = stale_kv[0]
    context_rows = stale_local.shape[1]
    results = []
    fresh_all = None
    previous = in_flight[0]
    for tick_number in range(micro_count):
        if tick_number == 0:
            current = previous
        else:
            current = from_behind(previous, "section", 1)
        patch_index = (tick_number - section_index) % micro_count
        entering = latents[tick_number]
        inputs = jnp.where(section_index == 0, entering, current)
        gathered = lax.all_gather(inputs, "sp", axis=0, tiled=True)
        modulated = modulate(gathered, shift_row, scale_row)
        patch_rows = modulated.shape[0]
        projected = jnp.dot(modulated, proj_weight, preferred_element_type=jnp.float32).reshape(
            patch_rows, 3, local_heads, head_dim
        )
        expanded = jnp.dot(modulated, expand_weight, preferred_element_type=jnp.float32)
        activated = jax.nn.gelu(expanded, approximate=True).astype(jnp.bfloat16)
        queries = head_norm(projected[:, 0], qk_gain[0, 0])
        key_rows = head_norm(projected[:, 1], qk_gain[0, 1])
        value_rows = projected[:, 2].astype(jnp.bfloat16)
        fresh_pair = jnp.stack(
            [key_rows.reshape(patch_rows, local_cols), value_rows.reshape(patch_rows, local_cols)],
            axis=0,
        )
        merged = lax.dynamic_update_slice_in_dim(
            stale_local, fresh_pair, patch_index * patch_rows, 1
        )
        all_keys = merged[0].reshape(context_rows, local_heads, head_dim)
        all_values = merged[1].reshape(context_rows, local_heads, head_dim)
        mixed_rows = attend(queries, all_keys, all_values, head_dim).reshape(patch_rows, local_cols)
        attn_part = jnp.dot(mixed_rows, out_weight, preferred_element_type=jnp.float32)
        hidden_part = jnp.dot(activated, contract_weight, preferred_element_type=jnp.float32)
        head_sum = lax.psum_scatter(
            (attn_part + hidden_part).astype(jnp.bfloat16), "sp", scatter_dimension=0, tiled=True
        ).astype(jnp.float32)
        result = (inputs.astype(jnp.float32) + gate_row * head_sum).astype(jnp.bfloat16)
        result, fresh_pair, patch_index = (result, fresh_pair, patch_index)
        if fresh_all is None:
            fresh_all = jnp.zeros((micro_count,) + fresh_pair.shape, jnp.bfloat16)
        fresh_all = lax.dynamic_update_index_in_dim(fresh_all, fresh_pair, patch_index, 0)
        results.append(result)
        previous = result
    section_out = jnp.stack(results, axis=0)
    return (section_out[None], fresh_all[None])


def solution(mesh):
    placed = (
        P(None, "sp", None),
        P("section", "sp", None),
        P("section", None, None),
        P("section", None, None, "sp"),
        P("section", None, "sp"),
        P("section", None, None),
        P("section", "sp", None),
        P("section", "sp", None),
        P("section", None, None, "sp"),
    )
    return jax.shard_map(
        local,
        mesh=mesh,
        in_specs=placed,
        out_specs=(P("section", None, "sp", None), P("section", None, None, None, "sp")),
        check_vma=False,
    )
```

profile of v0, /device:TPU:1, one launch (start us, length us, event | category | flops | bytes accessed | tf_op | source)
XLA Modules:
  0.0 685.9 jit_solution(3091980162340693309)
XLA Ops:
  11.7 4.3 copy.24
  16.0 58.8 %all-gather.12.cloned.1.call-done = bf16[1,256,3072]{2,1,0:T(8,128)(2,1)} async-done(((bf16[1,16,3072]{2,1,0:T(8,128)(2,1)}), bf16[1,256,3072]{2,1,0:T(8,128)(2,1)}) %all-gather.12.cloned.1.call-update) | async-done | bytes 1572880 | tf_op jit(solution)/shard_map/all_gather | solution.py:67
  78.7 2.7 fusion.55
  82.7 2.9 fusion.72
  85.6 8.7 %fusion.12 = bf16[256,3072]{1,0:T(8,128)(2,1)} fusion(f32[256,3072]{1,0:T(8,128)} %fusion.72, bf16[1,640,3072]{2,1,0:T(8,128)(2,1)} %param.16, bf16[1,3072,640]{2,1,0:T(8,128)(2,1)} %param.13, bf16[1,256,3072]{2,1,0:T(8,128)(2,1)} %all-gather.12.cloned.1.call-done, f32[3072]{0:T(1024)S(1)} %bitcast.303, f32[3072]{0:T(1024)S(1)} %bitcast.311, ...), kind=kOutput, calls=%fused_computation.24 | convolution fusion | flops 2021031936 | bytes 14182400 | tf_op jit(solution)/shard_map/dot_general | solution.py:89
  94.3 77.6 %reduce-scatter.5.cloned.1.call-done = bf16[16,3072]{1,0:T(8,128)(2,1)} async-done(((bf16[256,3072]{1,0:T(8,128)(2,1)}), bf16[16,3072]{1,0:T(8,128)(2,1)}) %reduce-scatter.5.cloned.1.call-update) | async-done | bytes 98320 | tf_op jit(solution)/shard_map/reduce_scatter | solution.py:90
  172.8 3.1 collective-permute-start
  179.4 59.3 %all-gather.6.cloned.1.call-done = bf16[256,3072]{1,0:T(8,128)(2,1)} async-done(((bf16[16,3072]{1,0:T(8,128)(2,1)}), bf16[256,3072]{1,0:T(8,128)(2,1)}) %all-gather.6.cloned.1.call-update) | async-done | bytes 1572880 | tf_op jit(solution)/shard_map/all_gather | solution.py:67
  243.1 2.7 fusion.61
  251.1 3.8 fusion.74
  255.0 8.1 %fusion.15 = bf16[256,3072]{1,0:T(8,128)(2,1)} fusion(f32[256,3072]{1,0:T(8,128)} %fusion.74, bf16[1,640,3072]{2,1,0:T(8,128)(2,1)} %param.16, bf16[1,3072,640]{2,1,0:T(8,128)(2,1)} %param.13, bf16[256,3072]{1,0:T(8,128)(2,1)S(1)} %copy-done.3, f32[256]{0:T(256)} %copy-done.47, f32[256]{0:T(256)} %copy-done.41, f32[3072]{0:T(1024)} %bitcast.300, ...), kind=kOutput, calls=%fused_computation.25 | convolution fusion | flops 2021031936 | bytes 14182400 | tf_op jit(solution)/shard_map/dot_general | solution.py:89
  263.2 77.6 %reduce-scatter.7.cloned.1.call-done = bf16[16,3072]{1,0:T(8,128)(2,1)} async-done(((bf16[256,3072]{1,0:T(8,128)(2,1)}), bf16[16,3072]{1,0:T(8,128)(2,1)}) %reduce-scatter.7.cloned.1.call-update) | async-done | bytes 98320 | tf_op jit(solution)/shard_map/reduce_scatter | solution.py:90
  341.7 3.1 collective-permute-start.1
  348.3 59.3 %all-gather.8.cloned.1.call-done = bf16[256,3072]{1,0:T(8,128)(2,1)} async-done(((bf16[16,3072]{1,0:T(8,128)(2,1)}), bf16[256,3072]{1,0:T(8,128)(2,1)}) %all-gather.8.cloned.1.call-update) | async-done | bytes 1572880 | tf_op jit(solution)/shard_map/all_gather | solution.py:67
  411.4 2.7 fusion.66
  419.4 3.8 fusion.76
  423.2 8.1 %fusion.18 = bf16[256,3072]{1,0:T(8,128)(2,1)} fusion(f32[256,3072]{1,0:T(8,128)} %fusion.76, bf16[1,640,3072]{2,1,0:T(8,128)(2,1)} %param.16, bf16[1,3072,640]{2,1,0:T(8,128)(2,1)} %param.13, bf16[256,3072]{1,0:T(8,128)(2,1)S(1)} %copy-done.4, f32[256]{0:T(256)} %copy-done.48, f32[256]{0:T(256)} %copy-done.42, f32[3072]{0:T(1024)} %bitcast.301, ...), kind=kOutput, calls=%fused_computation.26 | convolution fusion | flops 2021031936 | bytes 14182400 | tf_op jit(solution)/shard_map/dot_general | solution.py:89
  431.4 77.6 %reduce-scatter.9.cloned.1.call-done = bf16[16,3072]{1,0:T(8,128)(2,1)} async-done(((bf16[256,3072]{1,0:T(8,128)(2,1)}), bf16[16,3072]{1,0:T(8,128)(2,1)}) %reduce-scatter.9.cloned.1.call-update) | async-done | bytes 98320 | tf_op jit(solution)/shard_map/reduce_scatter | solution.py:90
  510.0 3.1 collective-permute-start.2
  516.6 59.2 %all-gather.10.cloned.1.call-done = bf16[256,3072]{1,0:T(8,128)(2,1)} async-done(((bf16[16,3072]{1,0:T(8,128)(2,1)}), bf16[256,3072]{1,0:T(8,128)(2,1)}) %all-gather.10.cloned.1.call-update) | async-done | bytes 1572880 | tf_op jit(solution)/shard_map/all_gather | solution.py:67
  579.7 2.7 fusion.49
  587.6 3.8 fusion.78
  591.4 8.2 %fusion.21 = bf16[256,3072]{1,0:T(8,128)(2,1)} fusion(f32[256,3072]{1,0:T(8,128)} %fusion.78, bf16[1,640,3072]{2,1,0:T(8,128)(2,1)} %param.16, bf16[1,3072,640]{2,1,0:T(8,128)(2,1)} %param.13, bf16[256,3072]{1,0:T(8,128)(2,1)S(1)} %copy-done.2, f32[256]{0:T(256)} %copy-done.46, f32[256]{0:T(256)S(1)} %copy-done.40, f32[3072]{0:T(1024)} %bitcast.302, ...), kind=kOutput, calls=%fused_computation.27 | convolution fusion | flops 2021031936 | bytes 14182400 | tf_op jit(solution)/shard_map/dot_general | solution.py:89
  600.8 76.5 %reduce-scatter.11.cloned.1.call-done = bf16[16,3072]{1,0:T(8,128)(2,1)} async-done(((bf16[256,3072]{1,0:T(8,128)(2,1)}), bf16[16,3072]{1,0:T(8,128)(2,1)}) %reduce-scatter.11.cloned.1.call-update) | async-done | bytes 98320 | tf_op jit(solution)/shard_map/reduce_scatter | solution.py:90
  (202 shorter events, 53.2 us)
Async XLA Ops:
  7.2 75.5 %copy-start = (bf16[1,128,3072]{2,1,0:T(8,128)(2,1)S(1)}, bf16[1,128,3072]{2,1,0:T(8,128)(2,1)}, u32[]{:S(2)}) copy-start(bf16[1,128,3072]{2,1,0:T(8,128)(2,1)} %param.15) | copy-start | bytes 2359300
  7.2 67.7 %all-gather.12.cloned.1.call-start = ((), (), s32[]{:S(2)}) async-start(), calls=%async_computation.11 | async-start | bytes 1671168 | tf_op jit(solution)/shard_map/all_gather | solution.py:67
  9.9 162.0 %reduce-scatter.5.cloned.1.call-start = ((), (), s32[]{:S(2)}) async-start(), calls=%async_computation.4 | async-start | bytes 1671168 | tf_op jit(solution)/shard_map/reduce_scatter | solution.py:90
  85.5 86.4 %copy-start.7 = (bf16[1,16,3072]{2,1,0:T(8,128)(2,1)S(1)}, bf16[1,16,3072]{2,1,0:T(8,128)(2,1)}, u32[]{:S(2)}) copy-start(bf16[1,16,3072]{2,1,0:T(8,128)(2,1)} %slice_select_fusion) | copy-start | bytes 294916
  94.2 144.5 %all-gather.6.cloned.1.call-start = ((), (), s32[]{:S(2)}) async-start(), calls=%async_computation.5 | async-start | bytes 1671168 | tf_op jit(solution)/shard_map/all_gather | solution.py:67
  172.8 4.7 collective-permute-start
  179.1 161.6 %reduce-scatter.7.cloned.1.call-start = ((), (), s32[]{:S(2)}) async-start(), calls=%async_computation.6 | async-start | bytes 1671168 | tf_op jit(solution)/shard_map/reduce_scatter | solution.py:90
  255.0 85.8 %copy-start.8 = (bf16[16,3072]{1,0:T(8,128)(2,1)S(1)}, bf16[16,3072]{1,0:T(8,128)(2,1)}, u32[]{:S(2)}) copy-start(bf16[16,3072]{1,0:T(8,128)(2,1)} %bitcast_select_fusion.2) | copy-start | bytes 294916
  263.1 148.3 %copy-start.30 = (f32[1,1,3072]{2,0,1:T(1,128)S(1)}, f32[1,1,3072]{2,0,1:T(1,128)}, u32[]{:S(2)}) copy-start(f32[1,1,3072]{2,0,1:T(1,128)} %copy-done.28) | copy-start | bytes 36868
  263.1 148.3 %copy-start.34 = (f32[1,1,3072]{2,0,1:T(1,128)S(1)}, f32[1,1,3072]{2,0,1:T(1,128)}, u32[]{:S(2)}) copy-start(f32[1,1,3072]{2,0,1:T(1,128)} %copy-done.32) | copy-start | bytes 36868
  263.1 144.4 %all-gather.8.cloned.1.call-start = ((), (), s32[]{:S(2)}) async-start(), calls=%async_computation.7 | async-start | bytes 1671168 | tf_op jit(solution)/shard_map/all_gather | solution.py:67
  341.7 4.7 collective-permute-start.1
  348.0 161.0 %reduce-scatter.9.cloned.1.call-start = ((), (), s32[]{:S(2)}) async-start(), calls=%async_computation.8 | async-start | bytes 1671168 | tf_op jit(solution)/shard_map/reduce_scatter | solution.py:90
  423.2 85.8 %copy-start.9 = (bf16[16,3072]{1,0:T(8,128)(2,1)S(1)}, bf16[16,3072]{1,0:T(8,128)(2,1)}, u32[]{:S(2)}) copy-start(bf16[16,3072]{1,0:T(8,128)(2,1)} %bitcast_select_fusion.1) | copy-start | bytes 294916
  431.3 148.3 %copy-start.31 = (f32[1,1,3072]{2,0,1:T(1,128)S(1)}, f32[1,1,3072]{2,0,1:T(1,128)}, u32[]{:S(2)}) copy-start(f32[1,1,3072]{2,0,1:T(1,128)} %copy-done.28) | copy-start | bytes 36868
  431.3 148.3 %copy-start.35 = (f32[1,1,3072]{2,0,1:T(1,128)S(1)}, f32[1,1,3072]{2,0,1:T(1,128)}, u32[]{:S(2)}) copy-start(f32[1,1,3072]{2,0,1:T(1,128)} %copy-done.32) | copy-start | bytes 36868
  431.4 144.4 %all-gather.10.cloned.1.call-start = ((), (), s32[]{:S(2)}) async-start(), calls=%async_computation.9 | async-start | bytes 1671168 | tf_op jit(solution)/shard_map/all_gather | solution.py:67
  510.0 4.7 collective-permute-start.2
  516.2 161.1 %reduce-scatter.11.cloned.1.call-start = ((), (), s32[]{:S(2)}) async-start(), calls=%async_computation.10 | async-start | bytes 1671168 | tf_op jit(solution)/shard_map/reduce_scatter | solution.py:90
  599.6 77.7 %copy-start.6 = (bf16[16,3072]{1,0:T(8,128)(2,1)S(1)}, bf16[16,3072]{1,0:T(8,128)(2,1)}, u32[]{:S(2)}) copy-start(bf16[16,3072]{1,0:T(8,128)(2,1)} %bitcast_select_fusion) | copy-start | bytes 294916
  599.6 78.7 %copy-start.18 = (bf16[16,3072]{1,0:T(8,128)(2,1)S(1)}, bf16[16,3072]{1,0:T(8,128)(2,1)}, u32[]{:S(2)}) copy-start(bf16[16,3072]{1,0:T(8,128)(2,1)} %copy-done.17) | copy-start | bytes 294916
  599.6 78.7 %copy-start.20 = (bf16[16,3072]{1,0:T(8,128)(2,1)S(1)}, bf16[16,3072]{1,0:T(8,128)(2,1)}, u32[]{:S(2)}) copy-start(bf16[16,3072]{1,0:T(8,128)(2,1)} %copy-done.19) | copy-start | bytes 294916
  599.6 78.7 %copy-start.22 = (bf16[16,3072]{1,0:T(8,128)(2,1)S(1)}, bf16[16,3072]{1,0:T(8,128)(2,1)}, u32[]{:S(2)}) copy-start(bf16[16,3072]{1,0:T(8,128)(2,1)} %copy-done.21) | copy-start | bytes 294916
  600.8 78.3 %copy-start.16 = (bf16[1,4,2,256,128]{4,3,2,1,0:T(8,128)(2,1)}, bf16[1,4,2,256,128]{4,3,2,1,0:T(8,128)(2,1)S(1)}, u32[]{:S(2)}) copy-start(bf16[1,4,2,256,128]{4,3,2,1,0:T(8,128)(2,1)S(1)} %constant_dynamic-update-slice_fusion) | copy-start | bytes 1572868
  (38 other events, 379.7 us)
Sparse Core Ops, SparseCore 0:
  11.3 63.5 all-gather.11
  94.4 77.4 reduce-scatter.4
  179.3 59.3 all-gather.5
  263.2 77.4 reduce-scatter.6
  348.1 59.4 all-gather.7
  431.5 77.4 reduce-scatter.8
  516.3 59.4 all-gather.9
  599.8 77.5 reduce-scatter.10
where the time goes:
time: 688 us; the launch traced here: 686 us
  waiting for transfers between devices  551 us (80%)
  matrix products  63.2 us (9%)
  other arithmetic  31.9 us (5%)
  between operations  15.1 us (2%)
  local copies, waits for them, and re-layouts  14.6 us (2%)
  starting transfers between devices  10.3 us (1%)
    reduce_scatter x4, waiting for transfers between devices, local(): lax.psum_scatter((attn_part + hidden_part).astype(jnp.bfloat16), 'sp', sc...  309 us
    all_gather x4, waiting for transfers between devices, local(): gathered = lax.all_gather(inputs, 'sp', axis=0, tiled=True)  237 us
    dot_general x4, matrix products, local(): jnp.dot(activated, contract_weight, preferred_element_type=jnp.float32)  33.1 us
    dot_general x4, matrix products, local(): jnp.dot(mixed_rows, out_weight, preferred_element_type=jnp.float32)  14.4 us
  transfers between devices with their start and end apart: 11, of which 11 were waited for; matrix products, arithmetic and copies ran while one was open for 1% of the time, Pallas kernels for 0%

commit v1 on v0

v1 whole, which is shorter than its diff:
```python
import jax
import jax.numpy as jnp
from jax import lax
from jax.experimental import pallas as pl
from jax.experimental.pallas import tpu as pltpu
from jax.sharding import PartitionSpec as P

MESH = pl.DeviceIdType.MESH
F32 = jnp.float32
BF16 = jnp.bfloat16
D = 3072
HD = 128
FFD = 640
ROWS = 16
PATCH = 256
CONTEXT = 1024
MICRO = 4
NSEC = 16
NC = 2
CW = D // NC
HALF = 128


def modulate(u, shift_row, scale_row):
    average = jnp.mean(u, axis=-1, keepdims=True)
    centred = u - average
    variance = jnp.mean(centred * centred, axis=-1, keepdims=True)
    normed = centred * lax.rsqrt(variance + 1e-06)
    return (normed * (1.0 + scale_row) + shift_row).astype(BF16)


def head_norm(values, gain_row):
    mean_square = jnp.mean(values * values, axis=-1, keepdims=True)
    return (values * lax.rsqrt(mean_square + 1e-06) * gain_row).astype(BF16)


def kernel(
    lat_ref, infl_ref, mod_ref, wqkv_ref, wexp_ref, gain_ref, wout_ref, wcon_ref, stale_ref,
    sec_ref, fresh_ref,
    win, wo, stale, kvw, lat, u_own, u_cur, mods, cat, q_buf, part, rx_d, r_buf, rx_y, t_buf, rx_x, ret_src, ret_rx,
    load_sem, iu_s, iu_r, lat_s, lat_r, ag_ys, ag_yr, ag_cs, ag_cr, rd_s, rd_r, ry_s, ry_r, x_s, x_r, ret_s, ret_r,
):
    s = lax.axis_index("section")
    p = lax.axis_index("sp")
    y = p // 4
    zh = lax.rem(p // 2, 2)
    c = lax.rem(p, 2)
    oc = 1 - c
    oz = 1 - zh
    s_next = lax.rem(s + 1, NSEC)
    s_prev = lax.rem(s + NSEC - 1, NSEC)

    def dev(section, yy, zz, cc):
        return {"section": section, "sp": (yy * 2 + zz) * 2 + cc}

    sibling = dev(s, y, zh, oc)
    zpart = dev(s, y, oz, c)
    ypeer = {d: dev(s, lax.rem(y + d, 4), zh, c) for d in (1, 2, 3)}
    nxt = (dev(s_next, y, zh, c), dev(s_next, y, oz, c))
    prv = (dev(s_prev, y, zh, c), dev(s_prev, y, oz, c))

    loads = [
        pltpu.make_async_copy(wqkv_ref, win.at[:, pl.ds(0, 3 * HD)], load_sem.at[0]),
        pltpu.make_async_copy(wexp_ref.at[0], win.at[:, pl.ds(3 * HD, FFD)], load_sem.at[1]),
        pltpu.make_async_copy(wout_ref.at[0], wo.at[pl.ds(0, HD)], load_sem.at[2]),
        pltpu.make_async_copy(wcon_ref.at[0], wo.at[pl.ds(HD, FFD)], load_sem.at[3]),
        pltpu.make_async_copy(stale_ref.at[0], stale, load_sem.at[4]),
    ]
    for load in loads:
        load.start()

    barrier = pltpu.get_barrier_semaphore()
    friends = [sibling, zpart, ypeer[1], ypeer[2], ypeer[3], nxt[0], nxt[1], prv[0], prv[1]]
    for friend in friends:
        pl.semaphore_signal(barrier, inc=1, device_id=friend, device_id_type=MESH)
    pl.semaphore_wait(barrier, len(friends))

    def remote(src, dst, ssem, rsem, target):
        return pltpu.make_async_remote_copy(
            src_ref=src, dst_ref=dst, send_sem=ssem, recv_sem=rsem, device_id=target, device_id_type=MESH
        )

    def c_init():
        return remote(u_own, u_cur.at[zh], iu_s, iu_r, zpart)

    def c_lat():
        return remote(lat.at[0], lat.at[1], lat_s, lat_r, zpart)

    def c_ag_y(j, z, d):
        slot = mods.at[j, z, c, y]
        return remote(slot, slot, ag_ys.at[j, z, d], ag_yr.at[j, z, d], ypeer[d])

    def c_ag_c(j, z, d):
        slot = mods.at[j, z, c, lax.rem(y + 4 - d, 4)]
        return remote(slot, slot, ag_cs.at[j, z, d], ag_cr.at[j, z, d], sibling)

    def cols(h):
        return pl.ds(h * CW, CW)

    def c_rd(j, z, h):
        return remote(
            part.at[z, oc, :, :, cols(h)], rx_d.at[j, z, :, :, cols(h)], rd_s.at[j, z, h], rd_r.at[j, z, h], sibling
        )

    def c_ry(j, z, h, d):
        return remote(
            r_buf.at[j, z, d, :, cols(h)], rx_y.at[j, z, d, :, cols(h)], ry_s.at[j, z, h, d], ry_r.at[j, z, h, d], ypeer[d]
        )

    def c_x(j, z, h, k):
        return remote(
            t_buf.at[j, z, :, cols(h)], rx_x.at[j, z, k, :, cols(h)], x_s.at[j, z, h, k], x_r.at[j, z, h, k], nxt[k]
        )

    def c_last(h):
        return remote(
            t_buf.at[MICRO - 1, oz, :, cols(h)], rx_x.at[MICRO - 1, 0, 1, :, cols(h)],
            x_s.at[MICRO - 1, 0, h, 1], x_r.at[MICRO - 1, 0, h, 1], zpart,
        )

    def c_ret(j):
        return remote(ret_src.at[j], ret_rx.at[j], ret_s.at[j], ret_r.at[j], prv[0])

    def norm_and_gather(j, z, u):
        mods[j, z, c, y] = modulate(u, mod_ref[0, 0:1], mod_ref[0, 1:2])
        for d in (2, 1, 3):
            c_ag_y(j, z, d).start()
        c_ag_c(j, z, 0).start()

    lat[0] = lat_ref[...]
    u_own[...] = jnp.where(s == 0, lat_ref[0], infl_ref[0])
    c_init().start()

    @pl.when(s == 0)
    def _():
        c_lat().start()

    u_cur[zh] = u_own[...]
    c_init().wait_recv()
    for z in range(2):
        norm_and_gather(0, z, u_cur[z].astype(F32))

    @pl.when(s == 0)
    def _():
        c_lat().wait_recv()

    for load in loads:
        load.wait()

    def body(j, carry):
        m = lax.rem(j - s + 2 * NSEC, MICRO)
        kvw[...] = stale[...]

        def gathered(z):
            for d in (1, 3, 2):
                c_ag_y(j, z, d).wait_recv()
                c_ag_c(j, z, d).start()
            for d in (0, 1, 3, 2):
                c_ag_c(j, z, d).wait_recv()

        def project(z):
            rows = mods[j, z].reshape(HALF, D)
            first = jnp.dot(rows, win[:, 0:512], preferred_element_type=F32)
            q_buf[z] = head_norm(first[:, 0:128], gain_ref[0, 0:1])
            keys = head_norm(first[:, 128:256], gain_ref[0, 1:2])
            values = first[:, 256:384].astype(BF16)
            for cc in range(2):
                for yy in range(4):
                    local_row = (cc * 4 + yy) * ROWS
                    row = yy * 64 + z * 32 + cc * 16
                    for k, new in ((0, keys), (1, values)):
                        block = new[local_row:local_row + ROWS]
                        kvw[k, pl.ds(pl.multiple_of(m * PATCH + row, ROWS), ROWS)] = block
                        fresh_ref[0, m, k, row:row + ROWS] = block
            cat[z, :, 128:256] = jax.nn.gelu(first[:, 384:512], approximate=True).astype(BF16)

        def expand(z):
            rows = mods[j, z].reshape(HALF, D)
            second = jnp.dot(rows, win[:, 512:1024], preferred_element_type=F32)
            cat[z, :, 256:768] = jax.nn.gelu(second, approximate=True).astype(BF16)

        def attend(z):
            scores = lax.dot_general(
                q_buf[z], kvw[0], (((1,), (1,)), ((), ())), preferred_element_type=F32
            ) * HD ** (-0.5)
            highest = jnp.max(scores, axis=-1, keepdims=True)
            weights = jnp.exp(scores - highest)
            totals = jnp.sum(weights, axis=-1, keepdims=True)
            shares = (weights / totals).astype(BF16)
            cat[z, :, 0:128] = jnp.dot(shares, kvw[1], preferred_element_type=F32).astype(BF16)

        def contract(z, h):
            product = jnp.dot(cat[z], wo[:, h * CW:(h + 1) * CW], preferred_element_type=F32)
            part[z, :, :, :, h * CW:(h + 1) * CW] = product.astype(BF16).reshape(2, 4, ROWS, CW)
            c_rd(j, z, h).start()

        def pair_sum(z, h):
            lo = h * CW
            c_rd(j, z, h).wait_recv()
            for d in (2, 1, 3):
                yy = lax.rem(y + d, 4)
                total = part[z, c, yy, :, lo:lo + CW].astype(F32) + rx_d[j, z, yy, :, lo:lo + CW].astype(F32)
                r_buf[j, z, d, :, lo:lo + CW] = total.astype(BF16)
                c_ry(j, z, h, d).start()

        def y_sum(z, h):
            lo = h * CW
            total = part[z, c, y, :, lo:lo + CW].astype(F32) + rx_d[j, z, y, :, lo:lo + CW].astype(F32)
            for d in (1, 3, 2):
                c_ry(j, z, h, d).wait_recv()
            for d in (1, 3, 2):
                total = total + rx_y[j, z, d, :, lo:lo + CW].astype(F32)
            total = total * mod_ref[0, 2:3, lo:lo + CW]
            base = u_cur[z, :, lo:lo + CW].astype(F32)
            total = total + jnp.where(zh == z, base, 0.0)
            t_buf[j, z, :, lo:lo + CW] = total.astype(BF16)

            @pl.when(j < MICRO - 1)
            def _():
                c_x(j, z, h, 1).start()
                c_x(j, z, h, 0).start()

        gathered(0)
        project(0)
        expand(0)
        gathered(1)
        project(1)
        attend(0)
        for h in range(NC):
            contract(0, h)
        expand(1)
        attend(1)
        for h in range(NC):
            pair_sum(0, h)
        for h in range(NC):
            contract(1, h)
        for h in range(NC):
            pair_sum(1, h)
        for z in range(2):
            for h in range(NC):
                y_sum(z, h)

        for z in range(2):
            for h in range(NC):
                c_rd(j, z, h).wait_send()

        @pl.when(j < MICRO - 1)
        def _():
            for z in range(2):
                for h in range(NC):
                    for k in range(2):
                        c_x(j, z, h, k).wait_recv()
                summed = (rx_x[j, z, 0].astype(F32) + rx_x[j, z, 1].astype(F32)).astype(BF16)

                @pl.when(zh == z)
                def _():
                    ret_src[j] = summed
                    c_ret(j).start()

                u_new = jnp.where(s == 0, jnp.where(zh == z, lat[0, j + 1], lat[1, j + 1]), summed)
                u_cur[z] = u_new
                norm_and_gather(j + 1, z, u_new.astype(F32))

        return carry

    lax.fori_loop(0, MICRO, body, 0)

    for h in range(NC):
        c_last(h).start()
    for h in range(NC):
        c_last(h).wait_recv()
    final = t_buf[MICRO - 1, zh].astype(F32) + rx_x[MICRO - 1, 0, 1].astype(F32)
    sec_ref[0, MICRO - 1] = final.astype(BF16)

    def finish(j, carry):
        c_ret(j).wait_recv()
        sec_ref[0, j] = ret_rx[j]
        c_ret(j).wait_send()
        for z in range(2):
            for h in range(NC):
                for k in range(2):
                    c_x(j, z, h, k).wait_send()
        return carry

    lax.fori_loop(0, MICRO - 1, finish, 0)

    def drain(j, carry):
        for z in range(2):
            for d in (1, 2, 3):
                c_ag_y(j, z, d).wait_send()
            for d in range(4):
                c_ag_c(j, z, d).wait_send()
            for h in range(NC):
                for d in (1, 2, 3):
                    c_ry(j, z, h, d).wait_send()
        return carry

    lax.fori_loop(0, MICRO, drain, 0)
    for h in range(NC):
        c_last(h).wait_send()
    c_init().wait_send()

    @pl.when(s == 0)
    def _():
        c_lat().wait_send()


def local(latents, in_flight, modulation, w_qkv, w_expand, qk_gain, w_out, w_contract, stale_kv):
    w_qkv = w_qkv[0].reshape(D, 3 * HD)
    vmem = pl.BlockSpec(memory_space=pltpu.VMEM)
    hbm = pl.BlockSpec(memory_space=pl.ANY)
    dma = pltpu.SemaphoreType.DMA
    return pl.pallas_call(
        kernel,
        out_shape=(
            jax.ShapeDtypeStruct((1, MICRO, ROWS, D), BF16),
            jax.ShapeDtypeStruct((1, MICRO, 2, PATCH, HD), BF16),
        ),
        in_specs=[vmem, vmem, vmem, hbm, hbm, vmem, hbm, hbm, hbm],
        out_specs=(vmem, vmem),
        scratch_shapes=[
            pltpu.VMEM((D, 3 * HD + FFD), BF16),
            pltpu.VMEM((HD + FFD, D), BF16),
            pltpu.VMEM((2, CONTEXT, HD), BF16),
            pltpu.VMEM((2, CONTEXT, HD), BF16),
            pltpu.VMEM((2, MICRO, ROWS, D), BF16),
            pltpu.VMEM((ROWS, D), BF16),
            pltpu.VMEM((2, ROWS, D), BF16),
            pltpu.VMEM((MICRO, 2, 2, 4, ROWS, D), BF16),
            pltpu.VMEM((2, HALF, HD + FFD), BF16),
            pltpu.VMEM((2, HALF, HD), BF16),
            pltpu.VMEM((2, 2, 4, ROWS, D), BF16),
            pltpu.VMEM((MICRO, 2, 4, ROWS, D), BF16),
            pltpu.VMEM((MICRO, 2, 4, ROWS, D), BF16),
            pltpu.VMEM((MICRO, 2, 4, ROWS, D), BF16),
            pltpu.VMEM((MICRO, 2, ROWS, D), BF16),
            pltpu.VMEM((MICRO, 2, 2, ROWS, D), BF16),
            pltpu.VMEM((MICRO - 1, ROWS, D), BF16),
            pltpu.VMEM((MICRO - 1, ROWS, D), BF16),
            dma((5,)),
            dma, dma, dma, dma,
            dma((MICRO, 2, 4)), dma((MICRO, 2, 4)),
            dma((MICRO, 2, 4)), dma((MICRO, 2, 4)),
            dma((MICRO, 2, NC)), dma((MICRO, 2, NC)),
            dma((MICRO, 2, NC, 4)), dma((MICRO, 2, NC, 4)),
            dma((MICRO, 2, NC, 2)), dma((MICRO, 2, NC, 2)),
            dma((MICRO - 1,)), dma((MICRO - 1,)),
        ],
        compiler_params=pltpu.CompilerParams(
            collective_id=0, has_side_effects=True, vmem_limit_bytes=60 * 2**20
        ),
        name="blocks",
    )(latents, in_flight, modulation, w_qkv, w_expand, qk_gain, w_out, w_contract, stale_kv)


def solution(mesh):
    placed = (
        P(None, "sp", None),
        P("section", "sp", None),
        P("section", None, None),
        P("section", None, None, "sp"),
        P("section", None, "sp"),
        P("section", None, None),
        P("section", "sp", None),
        P("section", "sp", None),
        P("section", None, None, "sp"),
    )
    return jax.shard_map(
        local,
        mesh=mesh,
        in_specs=placed,
        out_specs=(P("section", None, "sp", None), P("section", None, None, None, "sp")),
        check_vma=False,
    )
```

time: 688 us -> 156 us (0.23)
  waiting for transfers between devices: 551 us -> 0 us
  Pallas kernels: 0 us -> 145 us
  matrix products: 63.2 us -> 0 us
  other arithmetic: 31.9 us -> 0 us
  between operations: 15.1 us -> 0.66 us
  starting transfers between devices: 10.3 us -> 0 us
    reduce_scatter x4 -> x0, waiting for transfers between devices: 309 us -> none  [local(): lax.psum_scatter((attn_part + hidden_part).astype(jnp.bfloat16), 'sp', sc...]
    all_gather x4 -> x0, waiting for transfers between devices: 237 us -> none  [local(): gathered = lax.all_gather(inputs, 'sp', axis=0, tiled=True)]
    pallas_call x0 -> x1, Pallas kernels: none -> 145 us  [local(): pl.pallas_call(kernel, out_shape=(jax.ShapeDtypeStruct((1, MICRO, ROWS, D...]
    dot_general x16 -> x0, matrix products: 63.2 us -> none  [the longest x4 33.1 us: local(): jnp.dot(activated, contract_weight, preferred_element_type=jnp.float32)]
    reduce_sum x18 -> x0, other arithmetic: 18.2 us -> none  [the longest x4 7.84 us: modulate(): variance = jnp.mean(centred * centred, axis=-1, keepdims=True)]
    ppermute x3 -> x0, starting transfers between devices: 9.29 us -> none  [from_behind(): return lax.ppermute(block, axis, route)]
  transfers between devices with their start and end apart: 11 -> 0, of which waited for: 11 -> 0; matrix products, arithmetic and copies ran while one was open for 1% -> 0% of each run, Pallas kernels for 0% -> 0%
where the time goes in v1:
time: 156 us; the launch traced here: 155 us
  Pallas kernels  145 us (93%)
  local copies, waits for them, and re-layouts  9.57 us (6%)
    pallas_call x1, Pallas kernels, local(): pl.pallas_call(kernel, out_shape=(jax.ShapeDtypeStruct((1, MICRO, ROWS, D...  145 us
    unnamed x6, local copies, waits for them, and re-layouts  7.12 us

profile of v1, /device:TPU:1, one launch (start us, length us, event | category | flops | bytes accessed | tf_op | source)
XLA Modules:
  0.0 155.4 jit_solution(12916308118024203575)
XLA Ops:
  0.6 2.8 %copy.13 = bf16[1,3072,3,128]{1,3,2,0:T(8,128)(2,1)S(1)} copy(bf16[1,3072,3,128]{3,1,2,0:T(8,128)(2,1)} %param.12) | data formatting | bytes 4718592 | tf_op args[3]
  3.5 0.0 copy-start
  3.5 2.5 %copy.15.wqkv_ref = bf16[3072,384]{1,0:T(8,128)(2,1)} copy(bf16[3072,384]{0,1:T(8,128)(2,1)S(1)} %bitcast.1) | data formatting | bytes 4718592 | tf_op jit(solution)/shard_map/reshape;squeeze | solution.py:309
  5.9 0.0 copy-done
  5.9 0.6 copy.14.mod_ref
  6.6 145.2 %blocks.1 = (bf16[1,4,16,3072]{3,2,1,0:T(8,128)(2,1)}, bf16[1,4,2,256,128]{4,3,2,1,0:T(8,128)(2,1)}) custom-call(bf16[4,16,3072]{2,1,0:T(8,128)(2,1)} %lat_ref.1, bf16[1,16,3072]{2,1,0:T(8,128)(2,1)} %infl_ref.1, f32[1,3,3072]{2,1,0:T(4,128)} %copy.14.mod_ref, bf16[3072,384]{1,0:T(8,128)(2,1)} %copy.15.wqkv_ref, bf16[1,3072,640]{2,1,0:T(8,128)(2,1)} %wexp_ref.1, ...), custom_call_target="tpu_custom_call" | custom-call | tf_op jit(solution)/shard_map/blocks/pallas_call | solution.py:313
  151.8 1.8 %copy.18 = bf16[1,4,16,3072]{3,2,1,0:T(8,128)(2,1)} copy(bf16[1,4,16,3072]{3,2,1,0:T(8,128)(2,1)} %get-tuple-element.4) | data formatting | bytes 786432
  153.5 1.9 %copy.19 = bf16[1,4,2,256,128]{4,3,2,1,0:T(8,128)(2,1)} copy(bf16[1,4,2,256,128]{4,3,2,1,0:T(8,128)(2,1)} %get-tuple-element.5) | data formatting | bytes 1048576
Async XLA Ops:
  3.5 2.5 %copy-start = (f32[1,3,3072]{2,0,1:T(1,128)S(1)}, f32[1,3,3072]{2,0,1:T(1,128)}, u32[]{:S(2)}) copy-start(f32[1,3,3072]{2,0,1:T(1,128)} %param.11) | copy-start | bytes 110596

commit v2 on v1

v2 whole, which is shorter than its diff:
```python
import jax
import jax.numpy as jnp
from jax import lax
from jax.experimental import pallas as pl
from jax.experimental.pallas import tpu as pltpu
from jax.sharding import PartitionSpec as P

MESH = pl.DeviceIdType.MESH
F32 = jnp.float32
BF16 = jnp.bfloat16
D = 3072
HD = 128
FFD = 640
ROWS = 16
PATCH = 256
CONTEXT = 1024
MICRO = 4
NSEC = 16
NC = 2
CW = D // NC
GW = D // 2
HALF = 128


def modulate(u, shift_row, scale_row):
    average = jnp.mean(u, axis=-1, keepdims=True)
    centred = u - average
    variance = jnp.mean(centred * centred, axis=-1, keepdims=True)
    normed = centred * lax.rsqrt(variance + 1e-06)
    return (normed * (1.0 + scale_row) + shift_row).astype(BF16)


def head_norm(values, gain_row):
    mean_square = jnp.mean(values * values, axis=-1, keepdims=True)
    return (values * lax.rsqrt(mean_square + 1e-06) * gain_row).astype(BF16)


def kernel(
    lat_ref, infl_ref, mod_ref, wqkv_ref, wexp_ref, gain_ref, wout_ref, wcon_ref, stale_ref,
    sec_ref, fresh_ref,
    win, wo, stale, kvw, lat, u_own, mods, cat, hidden, q_buf, part, rx_d, r_buf, rx_y, t_buf, rx_x, ret_src, sec_buf, fresh_buf,
    load_sem, iu_s, iu_r, lat_s, lat_r, ag_ys, ag_yr, ag_cs, ag_cr, rd_s, rd_r, ry_s, ry_r, x_s, x_r, ret_s, ret_r, sec_sem, fresh_sem,
):
    s = lax.axis_index("section")
    p = lax.axis_index("sp")
    y = p // 4
    zh = lax.rem(p // 2, 2)
    c = lax.rem(p, 2)
    oc = 1 - c
    oz = 1 - zh
    s_next = lax.rem(s + 1, NSEC)
    s_prev = lax.rem(s + NSEC - 1, NSEC)

    def dev(section, yy, zz, cc):
        return {"section": section, "sp": (yy * 2 + zz) * 2 + cc}

    sibling = dev(s, y, zh, oc)
    zpart = dev(s, y, oz, c)
    up = dev(s, lax.rem(y + 1, 4), zh, c)
    down = dev(s, lax.rem(y + 3, 4), zh, c)
    far = dev(s, lax.rem(y + 2, 4), zh, c)
    nxt = (dev(s_next, y, zh, c), dev(s_next, y, oz, c))
    prv = (dev(s_prev, y, zh, c), dev(s_prev, y, oz, c))

    loads = [
        pltpu.make_async_copy(wqkv_ref.at[1], win.at[:, pl.ds(0, HD)], load_sem.at[0]),
        pltpu.make_async_copy(wqkv_ref.at[2], win.at[:, pl.ds(HD, HD)], load_sem.at[1]),
        pltpu.make_async_copy(wqkv_ref.at[0], win.at[:, pl.ds(2 * HD, HD)], load_sem.at[2]),
        pltpu.make_async_copy(wexp_ref.at[0], win.at[:, pl.ds(3 * HD, FFD)], load_sem.at[3]),
        pltpu.make_async_copy(wout_ref.at[0], wo.at[pl.ds(0, HD)], load_sem.at[4]),
        pltpu.make_async_copy(wcon_ref.at[0], wo.at[pl.ds(HD, FFD)], load_sem.at[5]),
        pltpu.make_async_copy(stale_ref.at[0], stale, load_sem.at[6]),
    ]
    for load in loads:
        load.start()

    barrier = pltpu.get_barrier_semaphore()
    friends = [sibling, zpart, up, down, far, nxt[0], nxt[1], prv[0], prv[1]]
    for friend in friends:
        pl.semaphore_signal(barrier, inc=1, device_id=friend, device_id_type=MESH)
    pl.semaphore_wait(barrier, len(friends))

    def remote(src, dst, ssem, rsem, target):
        return pltpu.make_async_remote_copy(
            src_ref=src, dst_ref=dst, send_sem=ssem, recv_sem=rsem, device_id=target, device_id_type=MESH
        )

    def c_init(g):
        half = mods.at[0, c, zh, y, :, pl.ds(g * GW, GW)]
        return remote(half, half, iu_s.at[g], iu_r.at[g], zpart)

    def c_lat():
        return remote(lat.at[0, pl.ds(1, MICRO - 1)], lat.at[1, pl.ds(1, MICRO - 1)], lat_s, lat_r, zpart)

    def c_ag_y(j, z, kind):
        half = mods.at[j, c, z, y, :, pl.ds((kind % 2) * GW, GW)]
        return remote(half, half, ag_ys.at[j, z, kind], ag_yr.at[j, z, kind], (far, up, down)[kind // 2])

    def c_ag_c(j, z, d):
        slot = mods.at[j, c, z, lax.rem(y + 4 - d, 4)]
        return remote(slot, slot, ag_cs.at[j, z, d], ag_cr.at[j, z, d], sibling)

    def cols(h):
        return pl.ds(h * CW, CW)

    def c_rd(j, z, h):
        return remote(
            part.at[oc, z, :, :, cols(h)], rx_d.at[j, z, :, :, cols(h)], rd_s.at[j, z, h], rd_r.at[j, z, h], sibling
        )

    def c_ry(j, z, h, d):
        return remote(
            r_buf.at[j, z, d, :, cols(h)], rx_y.at[j, z, d, :, cols(h)],
            ry_s.at[j, z, h, d], ry_r.at[j, z, h, d], {1: up, 2: far, 3: down}[d],
        )

    def c_x(j, z, h, k):
        return remote(
            t_buf.at[j, z, :, cols(h)], rx_x.at[j, z, k, :, cols(h)], x_s.at[j, z, h, k], x_r.at[j, z, h, k], nxt[k]
        )

    def c_last(h):
        return remote(
            t_buf.at[MICRO - 1, oz, :, cols(h)], rx_x.at[MICRO - 1, 0, 1, :, cols(h)],
            x_s.at[MICRO - 1, 0, h, 1], x_r.at[MICRO - 1, 0, h, 1], zpart,
        )

    def c_ret(j):
        return remote(ret_src.at[j], sec_buf.at[j], ret_s.at[j], ret_r.at[j], prv[0])

    def norm(j, z, u):
        mods[j, c, z, y] = modulate(u, mod_ref[0], mod_ref[1])

    def gather(j, z):
        for kind in range(6):
            c_ag_y(j, z, kind).start()
        c_ag_c(j, z, 0).start()

    lat[0] = lat_ref[...]
    u_own[...] = jnp.where(s == 0, lat_ref[0], infl_ref[0])
    norm(0, zh, u_own[...].astype(F32))
    for g in range(2):
        c_init(g).start()
    gather(0, zh)
    for g in range(2):
        c_init(g).wait_recv()
        for kind in (0, 2, 4):
            c_ag_y(0, oz, kind + g).start()
    c_ag_c(0, oz, 0).start()

    @pl.when(s == 0)
    def _():
        c_lat().start()

    for load in loads:
        load.wait()

    def body(j, carry):
        m = lax.rem(j - s + 2 * NSEC, MICRO)
        kvw[...] = stale[...]

        def forward(z):
            for d in (1, 3, 2):
                for g in range(2):
                    c_ag_y(j, z, {2: 0, 1: 2, 3: 4}[d] + g).wait_recv()
                c_ag_c(j, z, d).start()

        def gathered(k):
            @pl.when(c == k)
            def _():
                for z in range(2):
                    forward(z)

            @pl.when(c != k)
            def _():
                for z in range(2):
                    for d in (0, 1, 3, 2):
                        c_ag_c(j, z, d).wait_recv()

        def keys_values(k):
            rows = mods[j, k].reshape(HALF, D)
            pair = jnp.dot(rows, win[:, 0:256], preferred_element_type=F32)
            keys = head_norm(pair[:, 0:128], gain_ref[0, 1:2])
            values = pair[:, 128:256].astype(BF16)
            for z in range(2):
                for yy in range(4):
                    local_row = (z * 4 + yy) * ROWS
                    row = yy * 64 + z * 32 + k * 16
                    for i, new in ((0, keys), (1, values)):
                        block = new[local_row:local_row + ROWS]
                        kvw[i, pl.ds(pl.multiple_of(m * PATCH + row, ROWS), ROWS)] = block
                        fresh_buf[m, i, row:row + ROWS] = block

        def queries(k):
            rows = mods[j, k].reshape(HALF, D)
            pair = jnp.dot(rows, win[:, 256:512], preferred_element_type=F32)
            q_buf[k] = head_norm(pair[:, 0:128], gain_ref[0, 0:1])
            cat[k, :, 128:256] = jax.nn.gelu(pair[:, 128:256], approximate=True).astype(BF16)

        def expand(k):
            rows = mods[j, k].reshape(HALF, D)
            second = jnp.dot(rows, win[:, 512:1024], preferred_element_type=F32)
            cat[k, :, 256:768] = jax.nn.gelu(second, approximate=True).astype(BF16)

        def attend(k):
            scores = lax.dot_general(
                q_buf[k], kvw[0], (((1,), (1,)), ((), ())), preferred_element_type=F32
            ) * HD ** (-0.5)
            highest = jnp.max(scores, axis=-1, keepdims=True)
            weights = jnp.exp(scores - highest)
            totals = jnp.sum(weights, axis=-1, keepdims=True)
            shares = (weights / totals).astype(BF16)
            cat[k, :, 0:128] = jnp.dot(shares, kvw[1], preferred_element_type=F32).astype(BF16)

        def hidden_part():
            for h in range(NC):
                columns = slice(h * CW, (h + 1) * CW)
                hidden[:, columns] = jnp.dot(cat[0, :, HD:], wo[HD:, columns], preferred_element_type=F32)

        def contract(k, h):
            columns = slice(h * CW, (h + 1) * CW)

            def whole():
                product = jnp.dot(cat[k], wo[:, columns], preferred_element_type=F32)
                part[k, :, :, :, columns] = product.astype(BF16).reshape(2, 4, ROWS, CW)

            def rest():
                product = hidden[:, columns] + jnp.dot(
                    cat[k, :, 0:HD], wo[0:HD, columns], preferred_element_type=F32
                )
                part[k, :, :, :, columns] = product.astype(BF16).reshape(2, 4, ROWS, CW)

            if k == 0:
                pl.when(c == 0)(rest)
                pl.when(c == 1)(whole)
            else:
                whole()

            @pl.when(c != k)
            def _():
                for z in range(2):
                    c_rd(j, z, h).start()

        def pair_sum(z, h):
            lo = h * CW
            c_rd(j, z, h).wait_recv()
            for d in (2, 1, 3):
                yy = lax.rem(y + d, 4)
                r_buf[j, z, d, :, lo:lo + CW] = part[c, z, yy, :, lo:lo + CW] + rx_d[j, z, yy, :, lo:lo + CW]
                c_ry(j, z, h, d).start()

        def y_sum(z, h):
            lo = h * CW
            total = part[c, z, y, :, lo:lo + CW].astype(F32) + rx_d[j, z, y, :, lo:lo + CW].astype(F32)
            for d in (1, 3, 2):
                c_ry(j, z, h, d).wait_recv()
            for d in (1, 3, 2):
                total = total + rx_y[j, z, d, :, lo:lo + CW].astype(F32)
            total = total * mod_ref[2, :, lo:lo + CW]
            base = u_own[:, lo:lo + CW].astype(F32)
            total = total + jnp.where(zh == z, base, 0.0)
            t_buf[j, z, :, lo:lo + CW] = total.astype(BF16)

            @pl.when(j < MICRO - 1)
            def _():
                c_x(j, z, h, 1).start()
                c_x(j, z, h, 0).start()

            @pl.when(jnp.logical_and(j == MICRO - 1, oz == z))
            def _():
                c_last(h).start()

        def on_core(k, *steps):
            @pl.when(c == k)
            def _():
                for step, z, h in steps:
                    step(z, h)

        def on_core(k, *steps):
            @pl.when(c == k)
            def _():
                for step, z, h in steps:
                    step(z, h)

        gathered(0)
        @pl.when(c == 1)
        def _():
            forward(0)

        keys_values(0)
        queries(0)
        @pl.when(c == 1)
        def _():
            forward(1)

        expand(0)
        @pl.when(c == 0)
        def _():
            hidden_part()
            for z in range(2):
                for d in (0, 1, 3, 2):
                    c_ag_c(j, z, d).wait_recv()

        keys_values(1)
        attend(0)
        contract(0, 0)
        contract(0, 1)
        on_core(0, (pair_sum, 0, 0))
        queries(1)
        on_core(0, (pair_sum, 0, 1))
        expand(1)
        on_core(0, (pair_sum, 1, 0), (pair_sum, 1, 1))
        attend(1)
        contract(1, 0)
        on_core(0, (y_sum, 0, 0))
        contract(1, 1)
        on_core(0, (y_sum, 0, 1), (y_sum, 1, 0), (y_sum, 1, 1))
        on_core(1, (pair_sum, 0, 0), (pair_sum, 0, 1), (pair_sum, 1, 0), (pair_sum, 1, 1))
        on_core(1, (y_sum, 0, 0), (y_sum, 0, 1), (y_sum, 1, 0), (y_sum, 1, 1))

        def fresh_out():
            return pltpu.make_async_copy(fresh_buf.at[m], fresh_ref.at[0, m], fresh_sem.at[m])

        fresh_out().start()

        for z in range(2):
            for h in range(NC):
                c_rd(j, z, h).wait_send()

        @pl.when(jnp.logical_and(s == 0, j == 0))
        def _():
            c_lat().wait_recv()

        @pl.when(j < MICRO - 1)
        def _():
            for z in range(2):
                for h in range(NC):
                    for k in range(2):
                        c_x(j, z, h, k).wait_recv()
                summed = (rx_x[j, z, 0].astype(F32) + rx_x[j, z, 1].astype(F32)).astype(BF16)

                @pl.when(zh == z)
                def _():
                    ret_src[j] = summed
                    c_ret(j).start()

                u_new = jnp.where(s == 0, jnp.where(zh == z, lat[0, j + 1], lat[1, j + 1]), summed)

                @pl.when(zh == z)
                def _():
                    u_own[...] = u_new

                norm(j + 1, z, u_new.astype(F32))
                gather(j + 1, z)

        return carry

    lax.fori_loop(0, MICRO, body, 0)

    def sec_out(j):
        return pltpu.make_async_copy(sec_buf.at[j], sec_ref.at[0, j], sec_sem.at[j])

    for h in range(NC):
        lo = h * CW
        c_last(h).wait_recv()
        final = t_buf[MICRO - 1, zh, :, lo:lo + CW].astype(F32) + rx_x[MICRO - 1, 0, 1, :, lo:lo + CW].astype(F32)
        sec_buf[MICRO - 1, :, lo:lo + CW] = final.astype(BF16)
    sec_out(MICRO - 1).start()

    def finish(j, carry):
        c_ret(j).wait_recv()
        sec_out(j).start()
        c_ret(j).wait_send()
        for z in range(2):
            for h in range(NC):
                for k in range(2):
                    c_x(j, z, h, k).wait_send()
        return carry

    lax.fori_loop(0, MICRO - 1, finish, 0)

    def drain(j, carry):
        for z in range(2):
            for kind in range(6):
                c_ag_y(j, z, kind).wait_send()
            for d in range(4):
                c_ag_c(j, z, d).wait_send()
            for h in range(NC):
                for d in (1, 2, 3):
                    c_ry(j, z, h, d).wait_send()
        return carry

    lax.fori_loop(0, MICRO, drain, 0)
    for h in range(NC):
        c_last(h).wait_send()
    for j in range(MICRO):
        sec_out(j).wait()
        pltpu.make_async_copy(fresh_buf.at[j], fresh_ref.at[0, j], fresh_sem.at[j]).wait()
    for g in range(2):
        c_init(g).wait_send()

    @pl.when(s == 0)
    def _():
        c_lat().wait_send()


def place(sec_in, fresh_in, sec_out, fresh_out, sec_buf, fresh_buf, in_sem, out_sem):
    pairs = ((sec_in, sec_buf, sec_out), (fresh_in, fresh_buf, fresh_out))

    def arrive(k, j):
        return pltpu.make_async_copy(pairs[k][0].at[0, j], pairs[k][1].at[j], in_sem.at[k, j])

    def leave(k, j):
        return pltpu.make_async_copy(pairs[k][1].at[j], pairs[k][2].at[0, j], out_sem.at[k, j])

    steps = [(k, j) for j in range(MICRO) for k in range(2)]
    for step in steps:
        arrive(*step).start()
    for step in steps:
        arrive(*step).wait()
        leave(*step).start()
    for step in steps:
        leave(*step).wait()


def local(latents, in_flight, modulation, w_qkv, w_expand, qk_gain, w_out, w_contract, stale_kv):
    w_qkv = jnp.transpose(w_qkv[0], (1, 0, 2))
    modulation = jnp.transpose(modulation, (1, 0, 2))
    vmem = pl.BlockSpec(memory_space=pltpu.VMEM)
    hbm = pl.BlockSpec(memory_space=pl.ANY)
    dma = pltpu.SemaphoreType.DMA
    parts = pl.pallas_call(
        kernel,
        out_shape=(
            jax.ShapeDtypeStruct((1, MICRO, ROWS, D), BF16),
            jax.ShapeDtypeStruct((1, MICRO, 2, PATCH, HD), BF16),
        ),
        in_specs=[vmem, vmem, vmem, hbm, hbm, vmem, hbm, hbm, hbm],
        out_specs=(hbm, hbm),
        scratch_shapes=[
            pltpu.VMEM((D, 3 * HD + FFD), BF16),
            pltpu.VMEM((HD + FFD, D), BF16),
            pltpu.VMEM((2, CONTEXT, HD), BF16),
            pltpu.VMEM((2, CONTEXT, HD), BF16),
            pltpu.VMEM((2, MICRO, ROWS, D), BF16),
            pltpu.VMEM((ROWS, D), BF16),
            pltpu.VMEM((MICRO, 2, 2, 4, ROWS, D), BF16),
            pltpu.VMEM((2, HALF, HD + FFD), BF16),
            pltpu.VMEM((HALF, D), F32),
            pltpu.VMEM((2, HALF, HD), BF16),
            pltpu.VMEM((2, 2, 4, ROWS, D), BF16),
            pltpu.VMEM((MICRO, 2, 4, ROWS, D), BF16),
            pltpu.VMEM((MICRO, 2, 4, ROWS, D), BF16),
            pltpu.VMEM((MICRO, 2, 4, ROWS, D), BF16),
            pltpu.VMEM((MICRO, 2, ROWS, D), BF16),
            pltpu.VMEM((MICRO, 2, 2, ROWS, D), BF16),
            pltpu.VMEM((MICRO - 1, ROWS, D), BF16),
            pltpu.VMEM((MICRO, ROWS, D), BF16),
            pltpu.VMEM((MICRO, 2, PATCH, HD), BF16),
            dma((7,)),
            dma((2,)), dma((2,)), dma, dma,
            dma((MICRO, 2, 6)), dma((MICRO, 2, 6)),
            dma((MICRO, 2, 4)), dma((MICRO, 2, 4)),
            dma((MICRO, 2, NC)), dma((MICRO, 2, NC)),
            dma((MICRO, 2, NC, 4)), dma((MICRO, 2, NC, 4)),
            dma((MICRO, 2, NC, 2)), dma((MICRO, 2, NC, 2)),
            dma((MICRO - 1,)), dma((MICRO - 1,)),
            dma((MICRO,)), dma((MICRO,)),
        ],
        compiler_params=pltpu.CompilerParams(
            collective_id=0, has_side_effects=True, vmem_limit_bytes=60 * 2**20
        ),
        name="blocks",
    )(latents, in_flight, modulation, w_qkv, w_expand, qk_gain, w_out, w_contract, stale_kv)
    return pl.pallas_call(
        place,
        out_shape=tuple(jax.ShapeDtypeStruct(part.shape, part.dtype) for part in parts),
        in_specs=[hbm, hbm],
        out_specs=(hbm, hbm),
        scratch_shapes=[
            pltpu.VMEM((MICRO, ROWS, D), BF16),
            pltpu.VMEM((MICRO, 2, PATCH, HD), BF16),
            dma((2, MICRO)),
            dma((2, MICRO)),
        ],
        name="place",
    )(*parts)


def solution(mesh):
    placed = (
        P(None, "sp", None),
        P("section", "sp", None),
        P("section", None, None),
        P("section", None, None, "sp"),
        P("section", None, "sp"),
        P("section", None, None),
        P("section", "sp", None),
        P("section", "sp", None),
        P("section", None, None, "sp"),
    )
    return jax.shard_map(
        local,
        mesh=mesh,
        in_specs=placed,
        out_specs=(P("section", None, "sp", None), P("section", None, None, None, "sp")),
        check_vma=False,
    )
```

time: 156 us -> 137 us (0.88)
  Pallas kernels: 145 us -> 135 us
  local copies, waits for them, and re-layouts: 9.57 us -> 0 us
    pallas_call x1, Pallas kernels: 145 us -> 133 us  [local(): pl.pallas_call(kernel, out_shape=(jax.ShapeDtypeStruct((1, MICRO, ROWS, D...]
    unnamed x6 -> x0, local copies, waits for them, and re-layouts: 7.12 us -> none
    another operation x1 -> x0, local copies, waits for them, and re-layouts: 2.45 us -> none  [local(): w_qkv = w_qkv[0].reshape(D, 3 * HD)]
    pallas_call x0 -> x1, Pallas kernels: none -> 2.05 us  [local(): pl.pallas_call(place, out_shape=tuple((jax.ShapeDtypeStruct(part.shape, p...]
where the time goes in v2:
time: 137 us; the launch traced here: 135 us
  Pallas kernels  135 us (99%)
    pallas_call x1, Pallas kernels, local(): pl.pallas_call(kernel, out_shape=(jax.ShapeDtypeStruct((1, MICRO, ROWS, D...  133 us

profile of v2, /device:TPU:1, one launch (start us, length us, event | category | flops | bytes accessed | tf_op | source)
XLA Modules:
  0.0 135.5 jit_solution(3060399310127183504)
XLA Ops:
  0.6 132.8 %blocks.1 = (bf16[1,4,16,3072]{3,2,1,0:T(8,128)(2,1)}, bf16[1,4,2,256,128]{4,3,2,1,0:T(8,128)(2,1)}) custom-call(bf16[4,16,3072]{2,1,0:T(8,128)(2,1)} %lat_ref.1, bf16[1,16,3072]{2,1,0:T(8,128)(2,1)} %infl_ref.1, f32[3,1,3072]{2,1,0:T(1,128)} %bitcast.5, bf16[3,3072,128]{2,1,0:T(8,128)(2,1)} %bitcast.4, bf16[1,3072,640]{2,1,0:T(8,128)(2,1)} %wexp_ref.1, ...), custom_call_target="tpu_custom_call" | custom-call | tf_op jit(solution)/shard_map/blocks/pallas_call | solution.py:432
  133.4 2.0 %place.1 = (bf16[1,4,16,3072]{3,2,1,0:T(8,128)(2,1)}, bf16[1,4,2,256,128]{4,3,2,1,0:T(8,128)(2,1)}) custom-call(bf16[1,4,16,3072]{3,2,1,0:T(8,128)(2,1)} %get-tuple-element.4.sec_in, bf16[1,4,2,256,128]{4,3,2,1,0:T(8,128)(2,1)} %get-tuple-element.5.fresh_in), custom_call_target="tpu_custom_call" | custom-call | tf_op jit(solution)/shard_map/place/pallas_call | solution.py:475

commit v3 on v2

--- a/solution.py
+++ b/solution.py
@@ -20,6 +20,7 @@
 CW = D // NC
 GW = D // 2
 HALF = 128
+LOG2E = 1.4426950408889634
 
 
 def modulate(u, shift_row, scale_row):
@@ -78,7 +79,6 @@
     friends = [sibling, zpart, up, down, far, nxt[0], nxt[1], prv[0], prv[1]]
     for friend in friends:
         pl.semaphore_signal(barrier, inc=1, device_id=friend, device_id_type=MESH)
-    pl.semaphore_wait(barrier, len(friends))
 
     def remote(src, dst, ssem, rsem, target):
         return pltpu.make_async_remote_copy(
@@ -139,6 +139,7 @@
     lat[0] = lat_ref[...]
     u_own[...] = jnp.where(s == 0, lat_ref[0], infl_ref[0])
     norm(0, zh, u_own[...].astype(F32))
+    pl.semaphore_wait(barrier, len(friends))
     for g in range(2):
         c_init(g).start()
     gather(0, zh)
@@ -158,6 +159,10 @@
     def body(j, carry):
         m = lax.rem(j - s + 2 * NSEC, MICRO)
         kvw[...] = stale[...]
+        last = j // (MICRO - 1)
+
+        def ordered(z):
+            return (1 - last) * z + last * lax.rem(oz + z, 2)
 
         def forward(z):
             for d in (1, 3, 2):
@@ -205,11 +210,11 @@
         def attend(k):
             scores = lax.dot_general(
                 q_buf[k], kvw[0], (((1,), (1,)), ((), ())), preferred_element_type=F32
-            ) * HD ** (-0.5)
+            )
             highest = jnp.max(scores, axis=-1, keepdims=True)
-            weights = jnp.exp(scores - highest)
+            weights = jnp.exp2((scores - highest) * (HD ** (-0.5) * LOG2E))
             totals = jnp.sum(weights, axis=-1, keepdims=True)
-            shares = (weights / totals).astype(BF16)
+            shares = (weights * (1.0 / totals)).astype(BF16)
             cat[k, :, 0:128] = jnp.dot(shares, kvw[1], preferred_element_type=F32).astype(BF16)
 
         def hidden_part():
@@ -239,7 +244,7 @@
             @pl.when(c != k)
             def _():
                 for z in range(2):
-                    c_rd(j, z, h).start()
+                    c_rd(j, ordered(z), h).start()
 
         def pair_sum(z, h):
             lo = h * CW
@@ -263,8 +268,8 @@
 
             @pl.when(j < MICRO - 1)
             def _():
+                c_x(j, z, h, 0).start()
                 c_x(j, z, h, 1).start()
-                c_x(j, z, h, 0).start()
 
             @pl.when(jnp.logical_and(j == MICRO - 1, oz == z))
             def _():
@@ -274,13 +279,7 @@
             @pl.when(c == k)
             def _():
                 for step, z, h in steps:
-                    step(z, h)
-
-        def on_core(k, *steps):
-            @pl.when(c == k)
-            def _():
-                for step, z, h in steps:
-                    step(z, h)
+                    step(ordered(z), h)
 
         gathered(0)
         @pl.when(c == 1)
@@ -311,10 +310,11 @@
         expand(1)
         on_core(0, (pair_sum, 1, 0), (pair_sum, 1, 1))
         attend(1)
+        on_core(0, (y_sum, 0, 0))
         contract(1, 0)
-        on_core(0, (y_sum, 0, 0))
+        on_core(0, (y_sum, 0, 1))
         contract(1, 1)
-        on_core(0, (y_sum, 0, 1), (y_sum, 1, 0), (y_sum, 1, 1))
+        on_core(0, (y_sum, 1, 0), (y_sum, 1, 1))
         on_core(1, (pair_sum, 0, 0), (pair_sum, 0, 1), (pair_sum, 1, 0), (pair_sum, 1, 1))
         on_core(1, (y_sum, 0, 0), (y_sum, 0, 1), (y_sum, 1, 0), (y_sum, 1, 1))
 
@@ -339,19 +339,16 @@
                         c_x(j, z, h, k).wait_recv()
                 summed = (rx_x[j, z, 0].astype(F32) + rx_x[j, z, 1].astype(F32)).astype(BF16)
 
-                @pl.when(zh == z)
-                def _():
-                    ret_src[j] = summed
-                    c_ret(j).start()
-
                 u_new = jnp.where(s == 0, jnp.where(zh == z, lat[0, j + 1], lat[1, j + 1]), summed)
+
+                norm(j + 1, z, u_new.astype(F32))
+                gather(j + 1, z)
 
                 @pl.when(zh == z)
                 def _():
                     u_own[...] = u_new
-
-                norm(j + 1, z, u_new.astype(F32))
-                gather(j + 1, z)
+                    ret_src[j] = summed
+                    c_ret(j).start()
 
         return carry
 

time: 137 us -> 134 us (0.978)
  Pallas kernels: 135 us -> 133 us
    pallas_call x1, Pallas kernels: 133 us -> 131 us  [local(): pl.pallas_call(kernel, out_shape=(jax.ShapeDtypeStruct((1, MICRO, ROWS, D...]
where the time goes in v3:
time: 134 us; the launch traced here: 133 us
  Pallas kernels  133 us (99%)
    pallas_call x1, Pallas kernels, local(): pl.pallas_call(kernel, out_shape=(jax.ShapeDtypeStruct((1, MICRO, ROWS, D...  131 us

profile of v3, /device:TPU:1, one launch (start us, length us, event | category | flops | bytes accessed | tf_op | source)
XLA Modules:
  0.0 133.2 jit_solution(2118387831223388850)
XLA Ops:
  0.6 130.5 %blocks.1 = (bf16[1,4,16,3072]{3,2,1,0:T(8,128)(2,1)}, bf16[1,4,2,256,128]{4,3,2,1,0:T(8,128)(2,1)}) custom-call(bf16[4,16,3072]{2,1,0:T(8,128)(2,1)} %lat_ref.1, bf16[1,16,3072]{2,1,0:T(8,128)(2,1)} %infl_ref.1, f32[3,1,3072]{2,1,0:T(1,128)} %bitcast.5, bf16[3,3072,128]{2,1,0:T(8,128)(2,1)} %bitcast.4, bf16[1,3072,640]{2,1,0:T(8,128)(2,1)} %wexp_ref.1, ...), custom_call_target="tpu_custom_call" | custom-call | tf_op jit(solution)/shard_map/blocks/pallas_call | solution.py:429
  131.2 2.0 %place.1 = (bf16[1,4,16,3072]{3,2,1,0:T(8,128)(2,1)}, bf16[1,4,2,256,128]{4,3,2,1,0:T(8,128)(2,1)}) custom-call(bf16[1,4,16,3072]{3,2,1,0:T(8,128)(2,1)} %get-tuple-element.4.sec_in, bf16[1,4,2,256,128]{4,3,2,1,0:T(8,128)(2,1)} %get-tuple-element.5.fresh_in), custom_call_target="tpu_custom_call" | custom-call | tf_op jit(solution)/shard_map/place/pallas_call | solution.py:472
